TPU v7x, 256 devices: a whole 4x4x8 slice. The times are simulated.
256 devices in a mesh: seq: 32 (over z, y), head: 8 (over x, core).
Axes of the slice: x: 4, y: 4, z: 8, core: 2. Of those that a mesh axis runs over, the one named last changes fastest.
Arguments:
- cluster_id: int32 [32768], P(('seq', 'head')), may hold values from 0 to 255, as said below
- queries: bfloat16 [32768, 4096], P('seq', 'head'), may hold values from -6 to 6
- key_vectors: bfloat16 [32768, 4096], P('seq', 'head'), may hold values from -6 to 6
- value_vectors: bfloat16 [32768, 4096], P('seq', 'head'), may hold values from -6 to 6
- grad_output: bfloat16 [32768, 4096], P('seq', 'head'), may hold values from -6 to 6
Outputs:
- grad_query: bfloat16 [32768, 4096], P('seq', 'head')
- grad_key: bfloat16 [32768, 4096], P('seq', 'head')
- grad_value: bfloat16 [32768, 4096], P('seq', 'head')
Inputs may be any that keep to these rules, and one draw needn't show every extreme that they name: `cluster_id`: of the 1024 tokens of one index of seq, at most 48 have sorted positions in the block of 1024 sorted positions of any one index of seq, and some pair reaches 48 in every draw. The clusters of each block of 8 consecutive ids hold 1024 tokens together.
All inputs are finite; a program needn't handle non-finite values.
Results may differ from a plain program's by a relative error of at most 0.0093.
Values may be sent and summed in bfloat16 or wider, within the bound.
A program may use at most 128 MiB of HBM per device.

v0:
```python
import functools
import math

import jax
import jax.numpy as jnp
from jax import lax
from jax.experimental import pallas as pl
from jax.experimental.pallas import tpu as pltpu
from jax.sharding import PartitionSpec as P

MESH = pl.DeviceIdType.MESH
HD = 128
SPAN = 512
ROWS = 1024
SEQ = 32
HEAD = 8
NY = 4
NZ = 8
HEADS = 4
CAP = 32
DIRECT = SEQ * CAP
SIDE = 64
CROSS = 32
EXTRA = NY * SIDE
SLOTS = DIRECT + EXTRA
WIDE = 48
WIDE_SLOTS = SEQ * WIDE
QT = 256
FACTOR = 1.0 / math.sqrt(HD)
LOG2E = 1.4426950408889634
F32 = jnp.float32
BF16 = jnp.bfloat16
I32 = jnp.int32


def iota(shape, dim):
    return lax.broadcasted_iota(I32, shape, dim)


def onehot(mask):
    return jnp.where(mask, 1.0, 0.0).astype(BF16)


def mm(a, b):
    return jnp.dot(a, b, preferred_element_type=F32)


def mm_nt(a, b):
    return lax.dot_general(a, b, (((1,), (1,)), ((), ())), preferred_element_type=F32)


def aligned(value, size):
    return pl.multiple_of(value, size)


def column_hot(column, count):
    return jnp.concatenate(
        [onehot(column == iota((256, 128), 1) + 128 * c) for c in range(count)], axis=1
    )

def attend(rows, tail, grads, j, span, first):
    base = span * SPAN
    if span == 1:
        keys = rows[j, :, HD : 2 * HD]
        values = rows[j, :, 2 * HD : 3 * HD]
    else:
        keys = jnp.concatenate([tail[j, :, :HD], rows[j, :SPAN, HD : 2 * HD]], axis=0)
        values = jnp.concatenate([tail[j, :, HD:], rows[j, :SPAN, 2 * HD : 3 * HD]], axis=0)
    part_k = part_v = None
    for t in range(SPAN // QT):
        at = base + t * QT
        query = rows[j, at : at + QT, 0:HD]
        cot = rows[j, at : at + QT, 3 * HD : 4 * HD]
        scores = mm_nt(keys, query)
        if span == 0:
            gone = jnp.logical_and(iota((2 * SPAN, QT), 0) < SPAN, first)
            scores = jnp.where(gone, -jnp.inf, scores)
        top = jnp.max(scores, axis=0, keepdims=True)
        expo = jnp.exp2((scores - top) * (FACTOR * LOG2E))
        probs = expo * (1.0 / jnp.sum(expo, axis=0, keepdims=True))
        grad_probs = mm_nt(values, cot)
        delta = jnp.sum(probs * grad_probs, axis=0, keepdims=True)
        ds = (probs * (grad_probs - delta) * FACTOR).astype(BF16)
        pv = mm(probs.astype(BF16), cot)
        pk = mm(ds, query)
        part_k = pk if part_k is None else part_k + pk
        part_v = pv if part_v is None else part_v + pv
        dq = lax.dot_general(
            keys, ds, (((0,), (0,)), ((), ())), preferred_element_type=F32
        )
        grads[j, at : at + QT, 0:HD] = dq.T.astype(BF16)
    return part_k, part_v

def kernel(
    ids_ref, q_ref, k_ref, v_ref, g_ref, dq_ref, dk_ref, dv_ref, flag_ref,
    ids_buf, xin, send_f, recv_f, meta_s, meta_r, cnt_s, cnt_r, flag_s, flag_r, rows, tail,
    lead_s, lead_r, grads, send_r, recv_r, acc_k, acc_v, flat, send_row, send_col, pos_row,
    pos_col, spots, mb, mbt, mc, mct, a_r, b_s, b_r, c_s, cr_r, br_s, br_r, ar_s,
    in_sem, out_sem, ids_ss, ids_rs, meta_ss, meta_rs, cnt_ss, cnt_rs, flag_ss, flag_rs,
    fwd_ss, fwd_rs, ret_ss, ret_rs, tail_ss, tail_rs, lead_ss, lead_rs,
    a_ss, a_rs, b_ss, b_rs, c_ss, c_rs, cr_ss, cr_rs, br_ss, br_rs, ar_ss, ar_rs,
):
    me = lax.axis_index("seq")
    head = lax.axis_index("head")
    zi = me // NY
    yi = lax.rem(me, NY)

    def block_at(device, j):
        return (device // NY) * NY + lax.rem(lax.rem(device, NY) + NY - j, NY)

    def device_of(block, j):
        return (block // NY) * NY + lax.rem(lax.rem(block, NY) + j, NY)

    def peer(k):
        return lax.rem(me + k, SEQ)

    def remote(src, dst, ss, rs, seq, hd):
        return pltpu.make_async_remote_copy(
            src_ref=src, dst_ref=dst, send_sem=ss, recv_sem=rs,
            device_id=(seq, hd), device_id_type=MESH,
        )

    def wait_bytes(ref, sem):
        pltpu.make_async_copy(ref, ref, sem).wait()

    def in_copy(j, t):
        src = (q_ref, k_ref, v_ref, g_ref)[t]
        return pltpu.make_async_copy(
            src.at[:, pl.ds(aligned(j * HD, HD), HD)],
            xin.at[j, :, pl.ds(t * HD, HD)],
            in_sem.at[j, t],
        )

    def out_copy(j, t):
        dst = (dq_ref, dk_ref, dv_ref)[t]
        return pltpu.make_async_copy(
            xin.at[j, :, pl.ds(t * HD, HD)],
            dst.at[:, pl.ds(aligned(j * HD, HD), HD)],
            out_sem.at[j, t],
        )

    barrier = pltpu.get_barrier_semaphore()

    @pl.loop(1, SEQ)
    def _(k):
        pl.semaphore_signal(barrier, inc=1, device_id=(peer(k), head), device_id_type=MESH)

    @pl.loop(1, HEAD)
    def _(k):
        pl.semaphore_signal(
            barrier, inc=1, device_id=(me, lax.rem(head + k, HEAD)), device_id_type=MESH
        )

    @pl.loop(0, HEADS)
    def _(j):
        for t in range(4):
            in_copy(j, t).start()

    ids_buf[head] = ids_ref[...]
    pl.semaphore_wait(barrier, SEQ - 1 + HEAD - 1)

    @pl.loop(1, HEAD)
    def _(k):
        remote(
            ids_buf.at[head], ids_buf.at[head], ids_ss, ids_rs, me, lax.rem(head + k, HEAD)
        ).start()

    def slot_of(shape):
        col = iota(shape, 1)
        near = col < DIRECT
        past = col - DIRECT
        return (
            jnp.where(near, lax.shift_right_logical(col, 5), lax.shift_right_logical(past, 4)),
            jnp.where(near, col & 31, CAP + (past & 15)),
        )

    flat[...] = onehot(slot_of((128, DIRECT + 512))[1] == iota((128, DIRECT + 512), 0))
    upper = onehot(iota((128, 128), 0) < iota((128, 128), 1))
    sub = iota((SEQ, SEQ), 0)
    lan = iota((SEQ, SEQ), 1)
    below = onehot(lan < sub)
    below_z = onehot(
        jnp.logical_and(
            lan < sub, lax.shift_right_logical(lan, 2) == lax.shift_right_logical(sub, 2)
        )
    )
    row32 = iota((SEQ, 128), 0)
    row8 = iota((NZ, 128), 0)
    y_of = row32 & 3

    def quarter(value):
        return lax.shift_right_logical(value, 2)

    wait_bytes(ids_buf.at[pl.ds(0, HEAD - 1)], ids_rs)

    run = jnp.zeros((SEQ, 1), F32)
    owners, slots = [], []
    for c in range(ROWS // 128):
        owner = lax.shift_right_logical(ids_buf[c], 3)
        mine = jnp.where(row32 == owner, 1.0, 0.0)
        before = mm(mine.astype(BF16), upper) + run
        run = run + jnp.sum(mine, axis=1, keepdims=True)
        owners.append(owner)
        slots.append(jnp.sum(mine * before, axis=0, keepdims=True).astype(I32))

    past = jnp.maximum(jnp.broadcast_to(run, (SEQ, 128)) - float(CAP), 0.0)
    base_f = mm(below_z, past.astype(BF16))
    plane = onehot(quarter(iota((NZ, SEQ), 1)) == iota((NZ, SEQ), 0))
    cnt_s[...] = mm(plane, past.astype(BF16))
    cnt_r[yi] = cnt_s[...]

    @pl.loop(1, NY)
    def _(k):
        device = zi * NY + lax.rem(yi + k, NY)
        remote(cnt_s, cnt_r.at[yi], cnt_ss, cnt_rs, device, head).start()

    mine_e = cnt_s[...].astype(I32)
    offs = []
    for yy in range(NY):
        count = quarter(mine_e - ((yy - yi - row8 + 16) & 3) + 3).astype(F32)
        off = jnp.zeros((SEQ, 128), F32)
        for z in range(NZ - 1):
            off = off + jnp.where(quarter(row32) > z, count[z : z + 1, :], 0.0)
        offs.append(off)
    for c in range(ROWS // 128):
        owner, slot = owners[c], slots[c]
        mine = row32 == owner

        def pick(table):
            return jnp.sum(jnp.where(mine, table, 0.0), axis=0, keepdims=True).astype(I32)

        e = pick(base_f) + slot - CAP
        way = (e + yi + quarter(owner) + 64) & 3
        far = DIRECT + way * SIDE + quarter(e + 64) - 16
        for yy in range(NY):
            far = far + jnp.where(way == yy, pick(offs[yy]), 0)
        index = jnp.where(slot < CAP, owner * CAP + slot, far)
        send_row[:, c * 128 : (c + 1) * 128] = jnp.broadcast_to(index, (8, 128))

    def pack_tile(j, r0):
        choose = onehot(send_row[0:1, :] == iota((256, ROWS), 0) + r0)
        send_f[j, pl.ds(r0, 256), :] = mm(choose, xin[j]).astype(BF16)

    def y_peer(k):
        return lax.rem(yi + k, NY)

    def z_peer(k):
        return lax.rem(zi + k, NZ)

    def at_side(y):
        return pl.ds(aligned(y * SIDE, SIDE), SIDE)

    def at_cross(z):
        return pl.ds(aligned(z * CROSS, CROSS), CROSS)

    def at_extra(y):
        return pl.ds(aligned(DIRECT + y * SIDE, SIDE), SIDE)

    def stage_a(j):
        for t in range(4):
            in_copy(j, t).wait()
        pack_tile(j, DIRECT)

        @pl.loop(1, NY)
        def _(k):
            y = y_peer(k)
            remote(
                send_f.at[j, at_extra(y)], a_r.at[j, at_side(yi)], a_ss.at[j], a_rs.at[j],
                zi * NY + y, head,
            ).start()

        a_r[j, at_side(yi), :] = send_f[j, at_extra(yi), :]

    def stage_b(j):
        wait_bytes(a_r.at[j, pl.ds(0, EXTRA - SIDE)], a_rs.at[j])
        b_s[j] = mm(mb[...], a_r[j]).astype(BF16)

        @pl.loop(1, NZ)
        def _(k):
            z = z_peer(k)
            remote(
                b_s.at[j, at_cross(z)], b_r.at[j, at_cross(zi)], b_ss.at[j], b_rs.at[j],
                z * NY + yi, head,
            ).start()

        b_r[j, at_cross(zi), :] = b_s[j, at_cross(zi), :]

    def stage_c(j):
        wait_bytes(b_r.at[j, pl.ds(0, EXTRA - CROSS)], b_rs.at[j])
        c_s[j] = mm(mc[...], b_r[j]).astype(BF16)

        @pl.loop(1, NY)
        def _(k):
            y = y_peer(k)
            remote(
                c_s.at[j, at_side(lax.rem(y + NY - j, NY))], recv_f.at[j, at_extra(yi)],
                c_ss.at[j], c_rs.at[j], zi * NY + y, head,
            ).start()

        recv_f[j, at_extra(yi), :] = c_s[j, at_side(lax.rem(yi + NY - j, NY)), :]

    def pack_forward(j):
        @pl.loop(0, DIRECT // 256)
        def _(t):
            tile = lax.rem(zi // 2 + t, DIRECT // 256)
            pack_tile(j, aligned(tile * 256, 256))

            @pl.loop(0, 256 // CAP)
            def _(k):
                block = tile * (256 // CAP) + lax.rem(me + k, 256 // CAP)
                device = device_of(block, j)
                source = aligned(block * CAP, CAP)

                @pl.when(device != me)
                def _():
                    remote(
                        send_f.at[j, pl.ds(source, CAP)],
                        recv_f.at[j, pl.ds(aligned(me * CAP, CAP), CAP)],
                        fwd_ss.at[j], fwd_rs.at[j], device, head,
                    ).start()

        own = aligned(block_at(me, j) * CAP, CAP)
        recv_f[j, pl.ds(aligned(me * CAP, CAP), CAP), :] = send_f[j, pl.ds(own, CAP), :]

    stage_a(0)
    pack_forward(0)

    @pl.loop(1, HEADS)
    def _(j):
        stage_a(j)

    meta = jnp.zeros((SEQ, 128), F32)
    for c in range(ROWS // 128):
        cluster = (ids_buf[c] & 7).astype(F32) + 1.0
        mine = jnp.where(row32 == owners[c], cluster, 0.0)
        meta = meta + mm_nt(mine.astype(BF16), onehot(iota((128, 128), 0) == slots[c]))
    for b in range(SEQ):
        meta_s[b % NY, b // NY] = meta[b : b + 1, :]

    @pl.loop(1, SEQ)
    def _(k):
        device = peer(k)
        remote(
            meta_s.at[:, device // NY], meta_r.at[:, me], meta_ss, meta_rs, device, head
        ).start()

    for b in range(NY):
        meta_r[b, me] = meta_s[b, zi]
    wait_bytes(cnt_r.at[pl.ds(0, NY - 1)], cnt_rs)

    bad = jnp.zeros((1, 128), F32)
    starts_a, starts_b, counts = [], [], []
    filled = jnp.zeros((NZ, 128), I32)
    for y in range(NY):
        for yy in range(NY):
            share = quarter(cnt_r[y].astype(I32) - ((yy - y - row8 + 16) & 3) + 3)
            total = jnp.sum(share.astype(F32), axis=0, keepdims=True)
            bad = jnp.maximum(bad, total - float(SIDE))
        share = quarter(cnt_r[y].astype(I32) - ((yi - y - row8 + 16) & 3) + 3)
        start = jnp.zeros((NZ, 128), I32)
        for z in range(NZ - 1):
            start = start + jnp.where(row8 > z, share[z : z + 1, :], 0)
        starts_a.append(start)
        starts_b.append(filled)
        counts.append(share)
        filled = filled + share
    for yy in range(NY):
        total = jnp.zeros((NZ, 128), I32)
        for y in range(NY):
            total = total + quarter(cnt_r[y].astype(I32) - ((yy - y - row8 + 16) & 3) + 3)
        bad = jnp.maximum(
            bad, jnp.max(total.astype(F32), axis=0, keepdims=True) - float(CROSS)
        )

    def by_group(tables):
        group = lax.shift_right_logical(iota((NZ, EXTRA), 1), 6)
        result = jnp.zeros((NZ, EXTRA), I32)
        for y in range(NY):
            result = jnp.where(group == y, jnp.concatenate([tables[y]] * 2, axis=1), result)
        return result

    wide_a, wide_b, wide_c = by_group(starts_a), by_group(starts_b), by_group(counts)
    for z in range(NZ):
        step = iota((CROSS, EXTRA), 0) - wide_b[z : z + 1, :]
        place = (iota((CROSS, EXTRA), 1) & (SIDE - 1)) - wide_a[z : z + 1, :]
        hit = jnp.logical_and(
            jnp.logical_and(step >= 0, step < wide_c[z : z + 1, :]), step == place
        )
        mb[z * CROSS : (z + 1) * CROSS, :] = onehot(hit)
    mbt[...] = mb[...].astype(F32).T.astype(BF16)

    stage_b(0)
    pack_forward(1)

    @pl.loop(1, HEADS)
    def _(j):
        stage_b(j)

    for c in range(ROWS // 128):
        send_col[c * 128 : (c + 1) * 128, :] = (
            jnp.broadcast_to(send_row[0:1, c * 128 : (c + 1) * 128], (128, 128))
            .astype(F32).T.astype(I32)
        )
    wait_bytes(meta_r.at[:, pl.ds(0, SEQ - 1)], meta_rs)

    bases = [jnp.zeros((SEQ, 128), I32)]
    for b in range(NY):
        held = jnp.where(meta_r[b].reshape(SEQ, 128) > 0.5, 1.0, 0.0)
        held = jnp.maximum(jnp.sum(held, axis=1, keepdims=True) - float(CAP), 0.0)
        bases.append(bases[b] + jnp.broadcast_to(held, (SEQ, 128)).astype(I32))
    firsts = []
    for yy in range(NY):
        residue = (yy - y_of - zi + 16) & 3
        firsts.append([quarter(base - residue + 3) for base in bases])
    lengths = [[f[b + 1] - f[b] for b in range(NY)] for f in firsts]
    stacked = jnp.concatenate([v.astype(F32) for f in lengths for v in f], axis=1)
    before_c = mm(below, stacked.astype(BF16))
    landing = []
    for yy in range(NY):
        landing.append([])
        for b in range(NY):
            at = (yy * NY + b) * 128
            part = before_c[:, at : at + 128].astype(I32)
            landing[yy].append(part)
            total = (part + lengths[yy][b])[SEQ - 1 : SEQ, :].astype(F32)
            bad = jnp.maximum(bad, total - float(SIDE))
    lane = iota((SEQ, 128), 1)
    for b in range(NY):
        e = bases[b] + lane - CAP
        way = (e + y_of + zi + 64) & 3
        spot = jnp.zeros((SEQ, 128), I32)
        for yy in range(NY):
            here = yy * SIDE + landing[yy][b] + quarter(e + 64) - 16 - firsts[yy][b]
            spot = jnp.where(way == yy, here, spot)
        used = jnp.logical_and(meta_r[b].reshape(SEQ, 128) > 0.5, lane >= CAP)
        spots[b] = jnp.where(used, spot.astype(F32), -1.0)

    def chosen(tables):
        result = tables[0]
        for yy in range(1, NY):
            result = jnp.where(yi == yy, tables[yy], result)
        return result

    my_total = chosen([f[NY] for f in firsts])
    my_start = mm(below_z, my_total.astype(F32).astype(BF16))
    col = iota((SEQ, EXTRA), 1)
    for b in range(NY):
        landing_b = chosen([landing[yy][b] for yy in range(NY)]).astype(F32)
        length_b = chosen([lengths[yy][b] for yy in range(NY)]).astype(F32)
        source_b = my_start + chosen([firsts[yy][b] for yy in range(NY)]).astype(F32)
        found = jnp.zeros((SIDE, EXTRA), F32)
        for y in range(NY):
            match = iota((SEQ, EXTRA), 0) == lax.shift_right_logical(col, 5) * NY + y

            def across(table):
                twice = jnp.concatenate([table, table], axis=1)
                return jnp.sum(jnp.where(match, twice, 0.0), axis=0, keepdims=True).astype(I32)

            step = iota((SIDE, EXTRA), 0) - across(landing_b)
            place = (iota((SIDE, EXTRA), 1) & (CROSS - 1)) - across(source_b)
            hit = jnp.logical_and(
                jnp.logical_and(step >= 0, step < across(length_b)), step == place
            )
            found = found + jnp.where(hit, 1.0, 0.0)
        mc[b * SIDE : (b + 1) * SIDE, :] = found.astype(BF16)
    mct[...] = mc[...].astype(F32).T.astype(BF16)

    flag_s[...] = jnp.broadcast_to(jnp.where(bad > 0.5, 1.0, 0.0), (8, 128))
    flag_r[zi] = flag_s[...]

    @pl.loop(1, NZ)
    def _(k):
        remote(
            flag_s, flag_r.at[zi], flag_ss, flag_rs, z_peer(k) * NY + yi, head
        ).start()

    stage_c(0)

    def positions(j):
        block = lax.rem(yi + NY - j, NY)
        m = meta_r[block].reshape(SEQ, 128)
        hot = jnp.concatenate([jnp.where(m == c + 1.0, 1.0, 0.0) for c in range(8)], axis=0)
        within = mm(hot.astype(BF16), upper)
        total = jnp.broadcast_to(jnp.sum(hot, axis=1, keepdims=True), (8 * SEQ, 128))
        lower = onehot(iota((8 * SEQ, 8 * SEQ), 1) < iota((8 * SEQ, 8 * SEQ), 0))
        placed = hot * (mm(lower, total.astype(BF16)) + within)
        pos = jnp.where(m > 0.5, 0.0, -1.0)
        for c in range(8):
            pos = pos + placed[c * SEQ : (c + 1) * SEQ, :]

        def halves(value):
            high = jnp.floor(value * (1.0 / 32.0))
            return [high, value - high * 32.0]

        parts = mm(
            jnp.concatenate(halves(pos) + halves(spots[block]), axis=0).astype(BF16), flat[...]
        )
        mine = iota((SEQ, DIRECT + 512), 0) == slot_of((SEQ, DIRECT + 512))[0]
        spread = jnp.where(mine, parts[:SEQ] * 32.0 + parts[SEQ : 2 * SEQ], 0.0)
        line = jnp.sum(spread, axis=0, keepdims=True)
        spread = jnp.where(mine, parts[2 * SEQ : 3 * SEQ] * 32.0 + parts[3 * SEQ :], 0.0)
        target = jnp.sum(spread, axis=0, keepdims=True)[:, DIRECT:].astype(I32)
        high, low = halves(line[:, DIRECT:] + 1.0)
        pair = jnp.concatenate(
            [jnp.broadcast_to(high, (8, 512)), jnp.broadcast_to(low, (8, 512))], axis=0
        )
        found = mm_nt(pair.astype(BF16), onehot(iota((EXTRA, 512), 0) == target))
        extra = found[0:1, :] * 32.0 + found[8:9, :] - 1.0
        row = jnp.concatenate([line[:, :DIRECT], extra], axis=1)
        pos_row[j] = jnp.broadcast_to(row, (8, SLOTS)).astype(I32)
        for c in range(SLOTS // 128):
            piece = row[:, c * 128 : (c + 1) * 128]
            pos_col[j, c * 128 : (c + 1) * 128, :] = (
                jnp.broadcast_to(piece, (128, 128)).T.astype(I32)
            )

    def tail_copy(j):
        after = device_of(lax.rem(block_at(me, j) + 1, SEQ), j)
        return remote(
            rows.at[j, pl.ds(SPAN, SPAN), pl.ds(HD, 2 * HD)], tail.at[j],
            tail_ss.at[j], tail_rs.at[j], after, head,
        )

    def lead_copy(j):
        prior = device_of(lax.rem(block_at(me, j) + SEQ - 1, SEQ), j)
        return remote(lead_s.at[j], lead_r.at[j], lead_ss.at[j], lead_rs.at[j], prior, head)

    def open_chunk(j):
        positions(j)
        wait_bytes(recv_f.at[j, pl.ds(0, DIRECT - CAP)], fwd_rs.at[j])
        wait_bytes(recv_f.at[j, pl.ds(0, EXTRA - SIDE)], c_rs.at[j])

        @pl.loop(0, ROWS // 256)
        def _(t):
            r0 = aligned(t * 256, 256)
            choose = onehot(pos_row[j, 0:1, :] == iota((256, SLOTS), 0) + r0)
            rows[j, pl.ds(r0, 256), :] = mm(choose, recv_f[j]).astype(BF16)

        tail_copy(j).start()

    def last_span(j):
        part_k, part_v = attend(rows, tail, grads, j, 1, block_at(me, j) == 0)
        acc_k[j] = part_k
        acc_v[j] = part_v

    def first_span(j):
        tail_copy(j).wait_recv()
        part_k, part_v = attend(rows, tail, grads, j, 0, block_at(me, j) == 0)
        lead_s[j, :, :HD] = part_k[:SPAN].astype(BF16)
        lead_s[j, :, HD:] = part_v[:SPAN].astype(BF16)
        lead_copy(j).start()
        grads[j, :SPAN, HD : 2 * HD] = (acc_k[j, :SPAN] + part_k[SPAN:]).astype(BF16)
        grads[j, :SPAN, 2 * HD :] = (acc_v[j, :SPAN] + part_v[SPAN:]).astype(BF16)

    def back_b(j):
        wait_bytes(cr_r.at[j, pl.ds(0, EXTRA - SIDE)], cr_rs.at[j])
        br_s[j] = mm(mct[...], cr_r[j]).astype(BF16)

        @pl.loop(1, NZ)
        def _(k):
            z = z_peer(k)
            remote(
                br_s.at[j, at_cross(z)], br_r.at[j, at_cross(zi)], br_ss.at[j], br_rs.at[j],
                z * NY + yi, head,
            ).start()

        br_r[j, at_cross(zi), :] = br_s[j, at_cross(zi), :]

    def close_chunk(j):
        lead_copy(j).wait_recv()
        grads[j, SPAN:, HD : 2 * HD] = (
            acc_k[j, SPAN:] + lead_r[j, :, :HD].astype(F32)
        ).astype(BF16)
        grads[j, SPAN:, 2 * HD :] = (
            acc_v[j, SPAN:] + lead_r[j, :, HD:].astype(F32)
        ).astype(BF16)

        def pack_back(r0):
            choose = column_hot(pos_col[j, pl.ds(r0, 256), :], ROWS // 128)
            send_r[j, pl.ds(r0, 256), :] = mm(choose, grads[j]).astype(BF16)

        pack_back(DIRECT)
        own_y = lax.rem(yi + NY - j, NY)

        @pl.loop(1, NY)
        def _(k):
            y = y_peer(k)
            remote(
                send_r.at[j, at_extra(y)], cr_r.at[j, at_side(own_y)], cr_ss.at[j],
                cr_rs.at[j], zi * NY + y, head,
            ).start()

        cr_r[j, at_side(own_y), :] = send_r[j, at_extra(yi), :]

        @pl.loop(0, DIRECT // 256)
        def _(t):
            pack_back(aligned(t * 256, 256))

        own = aligned(block_at(me, j) * CAP, CAP)

        def send_back(k):
            device = peer(k)
            remote(
                send_r.at[j, pl.ds(aligned(device * CAP, CAP), CAP)],
                recv_r.at[j, pl.ds(own, CAP)],
                ret_ss.at[j], ret_rs.at[j], device, head,
            ).start()

        @pl.loop(1, SEQ // 2)
        def _(k):
            send_back(k)

        @pl.when(j == HEADS - 1)
        def _():
            back_b(j)

        @pl.loop(SEQ // 2, SEQ)
        def _(k):
            send_back(k)

        recv_r[j, pl.ds(own, CAP), :] = send_r[j, pl.ds(aligned(me * CAP, CAP), CAP), :]

    def back_a(j):
        wait_bytes(br_r.at[j, pl.ds(0, EXTRA - CROSS)], br_rs.at[j])
        ar_s[j] = mm(mbt[...], br_r[j]).astype(BF16)

        @pl.loop(1, NY)
        def _(k):
            y = y_peer(k)
            remote(
                ar_s.at[j, at_side(y)], recv_r.at[j, at_extra(yi)], ar_ss.at[j], ar_rs.at[j],
                zi * NY + y, head,
            ).start()

        recv_r[j, at_extra(yi), :] = ar_s[j, at_side(yi), :]

    @pl.loop(0, HEADS + 4)
    def _(i):
        @pl.when(i < HEADS)
        def _():
            open_chunk(i)

        @pl.when(jnp.logical_and(i >= 1, i <= HEADS))
        def _():
            first_span(i - 1)

        @pl.when(i < 1)
        def _():
            stage_c(1)

        @pl.when(i < HEADS - 2)
        def _():
            pack_forward(i + 2)
            stage_c(i + 2)

        @pl.when(i < HEADS)
        def _():
            last_span(i)

        @pl.when(jnp.logical_and(i >= 3, i < HEADS + 2))
        def _():
            back_b(i - 3)

        @pl.when(jnp.logical_and(i >= 2, i < HEADS + 2))
        def _():
            close_chunk(i - 2)

        @pl.when(i >= 4)
        def _():
            back_a(i - 4)

    @pl.loop(0, HEADS)
    def _(j):
        wait_bytes(recv_r.at[j, pl.ds(0, DIRECT - CAP)], ret_rs.at[j])
        wait_bytes(recv_r.at[j, pl.ds(0, EXTRA - SIDE)], ar_rs.at[j])

        @pl.loop(0, ROWS // 256)
        def _(t):
            r0 = aligned(t * 256, 256)
            choose = column_hot(send_col[pl.ds(r0, 256), :], SLOTS // 128)
            xin[j, pl.ds(r0, 256), : 3 * HD] = mm(choose, recv_r[j]).astype(BF16)

        for t in range(3):
            out_copy(j, t).start()

    wait_bytes(flag_r.at[pl.ds(0, NZ - 1)], flag_rs)
    flag_ref[0, 0] = jnp.max(flag_r[...])
    wait_bytes(ids_buf.at[pl.ds(0, HEAD - 1)], ids_ss)
    wait_bytes(meta_r.at[:, pl.ds(0, SEQ - 1)], meta_ss)
    wait_bytes(cnt_r.at[pl.ds(0, NY - 1)], cnt_ss)
    wait_bytes(flag_r.at[pl.ds(0, NZ - 1)], flag_ss)

    @pl.loop(0, HEADS)
    def _(j):
        wait_bytes(send_f.at[j, pl.ds(0, DIRECT - CAP)], fwd_ss.at[j])
        wait_bytes(send_r.at[j, pl.ds(0, DIRECT - CAP)], ret_ss.at[j])
        wait_bytes(a_r.at[j, pl.ds(0, EXTRA - SIDE)], a_ss.at[j])
        wait_bytes(b_r.at[j, pl.ds(0, EXTRA - CROSS)], b_ss.at[j])
        wait_bytes(c_s.at[j, pl.ds(0, EXTRA - SIDE)], c_ss.at[j])
        wait_bytes(cr_r.at[j, pl.ds(0, EXTRA - SIDE)], cr_ss.at[j])
        wait_bytes(br_r.at[j, pl.ds(0, EXTRA - CROSS)], br_ss.at[j])
        wait_bytes(ar_s.at[j, pl.ds(0, EXTRA - SIDE)], ar_ss.at[j])
        wait_bytes(tail.at[j], tail_ss.at[j])
        wait_bytes(lead_s.at[j], lead_ss.at[j])
        for t in range(3):
            out_copy(j, t).wait()


def wide_kernel(
    ids_ref, q_ref, k_ref, v_ref, g_ref, dq_ref, dk_ref, dv_ref,
    ids_buf, xin, send_f, recv_f, meta_s, meta_r, rows, tail, lead_s, lead_r,
    grads, send_r, recv_r, outs, acc_k, acc_v, flat, send_row, send_col, pos_row, pos_col,
    in_sem, out_sem, ids_ss, ids_rs, meta_ss, meta_rs, fwd_ss, fwd_rs, ret_ss, ret_rs,
    tail_ss, tail_rs, lead_ss, lead_rs,
):
    me = lax.axis_index("seq")
    head = lax.axis_index("head")
    zi = me // NY
    yi = lax.rem(me, NY)

    def block_at(device, j):
        return (device // NY) * NY + lax.rem(lax.rem(device, NY) + NY - j, NY)

    def device_of(block, j):
        return (block // NY) * NY + lax.rem(lax.rem(block, NY) + j, NY)

    def peer(k):
        return lax.rem(me + k, SEQ)

    def remote(src, dst, ss, rs, seq, hd):
        return pltpu.make_async_remote_copy(
            src_ref=src, dst_ref=dst, send_sem=ss, recv_sem=rs,
            device_id=(seq, hd), device_id_type=MESH,
        )

    def wait_bytes(ref, sem):
        pltpu.make_async_copy(ref, ref, sem).wait()

    def in_copy(j, t):
        src = (q_ref, k_ref, v_ref, g_ref)[t]
        return pltpu.make_async_copy(
            src.at[:, pl.ds(aligned(j * HD, HD), HD)],
            xin.at[j, :, pl.ds(t * HD, HD)],
            in_sem.at[j, t],
        )

    def out_copy(j, t):
        dst = (dq_ref, dk_ref, dv_ref)[t]
        return pltpu.make_async_copy(
            outs.at[j, :, pl.ds(t * HD, HD)],
            dst.at[:, pl.ds(aligned(j * HD, HD), HD)],
            out_sem.at[j, t],
        )

    barrier = pltpu.get_barrier_semaphore()

    @pl.loop(1, SEQ)
    def _(k):
        pl.semaphore_signal(barrier, inc=1, device_id=(peer(k), head), device_id_type=MESH)

    @pl.loop(1, HEAD)
    def _(k):
        pl.semaphore_signal(
            barrier, inc=1, device_id=(me, lax.rem(head + k, HEAD)), device_id_type=MESH
        )

    @pl.loop(0, HEADS)
    def _(j):
        for t in range(4):
            in_copy(j, t).start()

    ids_buf[head] = ids_ref[...]
    pl.semaphore_wait(barrier, SEQ - 1 + HEAD - 1)

    @pl.loop(1, HEAD)
    def _(k):
        remote(
            ids_buf.at[head], ids_buf.at[head], ids_ss, ids_rs, me, lax.rem(head + k, HEAD)
        ).start()

    lane = iota((128, WIDE_SLOTS), 1)
    source_of = lax.shift_right_logical(lane * 1366, 16)
    flat[...] = onehot(lane - source_of * WIDE == iota((128, WIDE_SLOTS), 0))
    upper = onehot(iota((128, 128), 0) < iota((128, 128), 1))
    wait_bytes(ids_buf.at[pl.ds(0, HEAD - 1)], ids_rs)

    run = jnp.zeros((SEQ, 1), F32)
    meta = jnp.zeros((SEQ, 128), F32)
    for c in range(ROWS // 128):
        idc = ids_buf[c]
        owner = lax.shift_right_logical(idc, 3)
        cluster = (idc & 7).astype(F32) + 1.0
        mine = jnp.where(iota((SEQ, 128), 0) == owner, 1.0, 0.0)
        before = mm(mine.astype(BF16), upper) + run
        run = run + jnp.sum(mine, axis=1, keepdims=True)
        slot = jnp.sum(mine * before, axis=0, keepdims=True).astype(I32)
        index = owner * WIDE + slot
        send_row[:, c * 128 : (c + 1) * 128] = jnp.broadcast_to(index, (8, 128))
        send_col[c * 128 : (c + 1) * 128, :] = (
            jnp.broadcast_to(index, (128, 128)).astype(F32).T.astype(I32)
        )
        meta = meta + mm_nt((mine * cluster).astype(BF16), onehot(iota((128, 128), 0) == slot))
    for b in range(SEQ):
        meta_s[b % NY, b // NY] = meta[b : b + 1, :]

    @pl.loop(1, SEQ)
    def _(k):
        device = peer(k)
        remote(
            meta_s.at[:, device // NY], meta_r.at[:, me], meta_ss, meta_rs, device, head
        ).start()

    for b in range(NY):
        meta_r[b, me] = meta_s[b, zi]

    def pack_forward(j):
        for t in range(4):
            in_copy(j, t).wait()

        @pl.loop(0, WIDE_SLOTS // 256)
        def _(t):
            r0 = aligned(t * 256, 256)
            choose = onehot(send_row[0:1, :] == iota((256, ROWS), 0) + r0)
            send_f[j, pl.ds(r0, 256), :] = mm(choose, xin[j]).astype(BF16)

        @pl.loop(1, SEQ)
        def _(k):
            device = peer(k)
            start = aligned(block_at(device, j) * WIDE, WIDE)
            remote(
                send_f.at[j, pl.ds(start, WIDE)],
                recv_f.at[j, pl.ds(aligned(me * WIDE, WIDE), WIDE)],
                fwd_ss.at[j], fwd_rs.at[j], device, head,
            ).start()

        own = aligned(block_at(me, j) * WIDE, WIDE)
        recv_f[j, pl.ds(aligned(me * WIDE, WIDE), WIDE), :] = send_f[j, pl.ds(own, WIDE), :]

    @pl.loop(0, 2)
    def _(j):
        pack_forward(j)

    wait_bytes(meta_r.at[:, pl.ds(0, SEQ - 1)], meta_rs)

    def positions(j):
        m = meta_r[lax.rem(yi + NY - j, NY)].reshape(SEQ, 128)
        hot = jnp.concatenate([jnp.where(m == c + 1.0, 1.0, 0.0) for c in range(8)], axis=0)
        within = mm(hot.astype(BF16), upper)
        total = jnp.broadcast_to(jnp.sum(hot, axis=1, keepdims=True), (8 * SEQ, 128))
        lower = onehot(iota((8 * SEQ, 8 * SEQ), 1) < iota((8 * SEQ, 8 * SEQ), 0))
        placed = hot * (mm(lower, total.astype(BF16)) + within)
        pos = jnp.where(m > 0.5, 0.0, -1.0)
        for c in range(8):
            pos = pos + placed[c * SEQ : (c + 1) * SEQ, :]
        high = jnp.floor(pos * (1.0 / 32.0))
        low = pos - high * 32.0
        parts = mm(jnp.concatenate([high, low], axis=0).astype(BF16), flat[...])
        spread = parts[:SEQ] * 32.0 + parts[SEQ:]
        mine = iota((SEQ, WIDE_SLOTS), 0) == lax.shift_right_logical(iota((SEQ, WIDE_SLOTS), 1) * 1366, 16)
        row = jnp.sum(jnp.where(mine, spread, 0.0), axis=0, keepdims=True)
        pos_row[j] = jnp.broadcast_to(row, (8, WIDE_SLOTS)).astype(I32)
        for c in range(WIDE_SLOTS // 128):
            piece = row[:, c * 128 : (c + 1) * 128]
            pos_col[j, c * 128 : (c + 1) * 128, :] = (
                jnp.broadcast_to(piece, (128, 128)).T.astype(I32)
            )

    def tail_copy(j):
        after = device_of(lax.rem(block_at(me, j) + 1, SEQ), j)
        return remote(
            rows.at[j, pl.ds(SPAN, SPAN), pl.ds(HD, 2 * HD)], tail.at[j],
            tail_ss.at[j], tail_rs.at[j], after, head,
        )

    def lead_copy(j):
        prior = device_of(lax.rem(block_at(me, j) + SEQ - 1, SEQ), j)
        return remote(lead_s.at[j], lead_r.at[j], lead_ss.at[j], lead_rs.at[j], prior, head)

    def open_chunk(j):
        positions(j)
        wait_bytes(recv_f.at[j, pl.ds(0, WIDE_SLOTS - WIDE)], fwd_rs.at[j])

        @pl.loop(0, ROWS // 256)
        def _(t):
            r0 = aligned(t * 256, 256)
            choose = onehot(pos_row[j, 0:1, :] == iota((256, WIDE_SLOTS), 0) + r0)
            rows[j, pl.ds(r0, 256), :] = mm(choose, recv_f[j]).astype(BF16)

        tail_copy(j).start()

    def last_span(j):
        part_k, part_v = attend(rows, tail, grads, j, 1, block_at(me, j) == 0)
        acc_k[j] = part_k
        acc_v[j] = part_v

    def first_span(j):
        tail_copy(j).wait_recv()
        part_k, part_v = attend(rows, tail, grads, j, 0, block_at(me, j) == 0)
        lead_s[j, :, :HD] = part_k[:SPAN].astype(BF16)
        lead_s[j, :, HD:] = part_v[:SPAN].astype(BF16)
        lead_copy(j).start()
        grads[j, :SPAN, HD : 2 * HD] = (acc_k[j, :SPAN] + part_k[SPAN:]).astype(BF16)
        grads[j, :SPAN, 2 * HD :] = (acc_v[j, :SPAN] + part_v[SPAN:]).astype(BF16)

    def close_chunk(j):
        lead_copy(j).wait_recv()
        grads[j, SPAN:, HD : 2 * HD] = (
            acc_k[j, SPAN:] + lead_r[j, :, :HD].astype(F32)
        ).astype(BF16)
        grads[j, SPAN:, 2 * HD :] = (
            acc_v[j, SPAN:] + lead_r[j, :, HD:].astype(F32)
        ).astype(BF16)

        @pl.loop(0, WIDE_SLOTS // 256)
        def _(t):
            r0 = aligned(t * 256, 256)
            choose = column_hot(pos_col[j, pl.ds(r0, 256), :], ROWS // 128)
            send_r[j, pl.ds(r0, 256), :] = mm(choose, grads[j]).astype(BF16)

        own = aligned(block_at(me, j) * WIDE, WIDE)

        @pl.loop(1, SEQ)
        def _(k):
            device = peer(k)
            remote(
                send_r.at[j, pl.ds(aligned(device * WIDE, WIDE), WIDE)],
                recv_r.at[j, pl.ds(own, WIDE)],
                ret_ss.at[j], ret_rs.at[j], device, head,
            ).start()

        recv_r[j, pl.ds(own, WIDE), :] = send_r[j, pl.ds(aligned(me * WIDE, WIDE), WIDE), :]

    @pl.loop(0, HEADS + 2)
    def _(i):
        @pl.when(i < HEADS)
        def _():
            open_chunk(i)

        @pl.when(i < HEADS - 2)
        def _():
            pack_forward(i + 2)

        @pl.when(jnp.logical_and(i >= 1, i <= HEADS))
        def _():
            first_span(i - 1)

        @pl.when(i < HEADS)
        def _():
            last_span(i)

        @pl.when(i >= 2)
        def _():
            close_chunk(i - 2)

    @pl.loop(0, HEADS)
    def _(j):
        wait_bytes(recv_r.at[j, pl.ds(0, WIDE_SLOTS - WIDE)], ret_rs.at[j])

        @pl.loop(0, ROWS // 256)
        def _(t):
            r0 = aligned(t * 256, 256)
            choose = column_hot(send_col[pl.ds(r0, 256), :], WIDE_SLOTS // 128)
            outs[j, pl.ds(r0, 256), :] = mm(choose, recv_r[j]).astype(BF16)

        for t in range(3):
            out_copy(j, t).start()

    wait_bytes(ids_buf.at[pl.ds(0, HEAD - 1)], ids_ss)
    wait_bytes(meta_r.at[:, pl.ds(0, SEQ - 1)], meta_ss)

    @pl.loop(0, HEADS)
    def _(j):
        wait_bytes(send_f.at[j, pl.ds(0, WIDE_SLOTS - WIDE)], fwd_ss.at[j])
        wait_bytes(send_r.at[j, pl.ds(0, WIDE_SLOTS - WIDE)], ret_ss.at[j])
        wait_bytes(tail.at[j], tail_ss.at[j])
        wait_bytes(lead_s.at[j], lead_ss.at[j])
        for t in range(3):
            out_copy(j, t).wait()


def call_kernel(args):
    hbm = pl.BlockSpec(memory_space=pl.ANY)
    near = pl.BlockSpec(memory_space=pltpu.VMEM)
    dma = pltpu.SemaphoreType.DMA
    grad = jax.ShapeDtypeStruct((ROWS, HEADS * HD), BF16)
    step = pltpu.VMEM((HEADS, EXTRA, 4 * HD), BF16)
    back = pltpu.VMEM((HEADS, EXTRA, 3 * HD), BF16)
    square = pltpu.VMEM((EXTRA, EXTRA), BF16)
    return pl.pallas_call(
        kernel,
        out_shape=(grad, grad, grad, jax.ShapeDtypeStruct((1, 1), F32)),
        in_specs=[near, hbm, hbm, hbm, hbm],
        out_specs=(hbm, hbm, hbm, pl.BlockSpec(memory_space=pltpu.SMEM)),
        scratch_shapes=[
            pltpu.VMEM((HEAD, 1, 128), I32),
            pltpu.VMEM((HEADS, ROWS, 4 * HD), BF16),
            pltpu.VMEM((HEADS, SLOTS, 4 * HD), BF16),
            pltpu.VMEM((HEADS, SLOTS, 4 * HD), BF16),
            pltpu.VMEM((NY, NZ, 1, 128), F32),
            pltpu.VMEM((NY, SEQ, 1, 128), F32),
            pltpu.VMEM((NZ, 128), F32),
            pltpu.VMEM((NY, NZ, 128), F32),
            pltpu.VMEM((8, 128), F32),
            pltpu.VMEM((NZ, 8, 128), F32),
            pltpu.VMEM((HEADS, ROWS, 4 * HD), BF16),
            pltpu.VMEM((HEADS, SPAN, 2 * HD), BF16),
            pltpu.VMEM((HEADS, SPAN, 2 * HD), BF16),
            pltpu.VMEM((HEADS, SPAN, 2 * HD), BF16),
            pltpu.VMEM((HEADS, ROWS, 3 * HD), BF16),
            pltpu.VMEM((HEADS, SLOTS, 3 * HD), BF16),
            pltpu.VMEM((HEADS, SLOTS, 3 * HD), BF16),
            pltpu.VMEM((HEADS, ROWS, HD), F32),
            pltpu.VMEM((HEADS, ROWS, HD), F32),
            pltpu.VMEM((128, DIRECT + 512), BF16),
            pltpu.VMEM((8, ROWS), I32),
            pltpu.VMEM((ROWS, 128), I32),
            pltpu.VMEM((HEADS, 8, SLOTS), I32),
            pltpu.VMEM((HEADS, SLOTS, 128), I32),
            pltpu.VMEM((NY, SEQ, 128), F32),
            square, square, square, square,
            step, step, step, step, back, back, back, back,
            dma((HEADS, 4)),
            dma((HEADS, 3)),
        ]
        + [dma] * 8
        + [dma((HEADS,))] * 20,
        compiler_params=pltpu.CompilerParams(
            collective_id=0, has_side_effects=True, vmem_limit_bytes=60 * 1024 * 1024
        ),
    )(*args)


def call_wide(args):
    hbm = pl.BlockSpec(memory_space=pl.ANY)
    dma = pltpu.SemaphoreType.DMA
    grad = jax.ShapeDtypeStruct((ROWS, HEADS * HD), BF16)
    return pl.pallas_call(
        wide_kernel,
        out_shape=(grad, grad, grad),
        in_specs=[pl.BlockSpec(memory_space=pltpu.VMEM), hbm, hbm, hbm, hbm],
        out_specs=(hbm, hbm, hbm),
        scratch_shapes=[
            pltpu.VMEM((HEAD, 1, 128), I32),
            pltpu.VMEM((HEADS, ROWS, 4 * HD), BF16),
            pltpu.VMEM((HEADS, WIDE_SLOTS, 4 * HD), BF16),
            pltpu.VMEM((HEADS, WIDE_SLOTS, 4 * HD), BF16),
            pltpu.VMEM((NY, NZ, 1, 128), F32),
            pltpu.VMEM((NY, SEQ, 1, 128), F32),
            pltpu.VMEM((HEADS, ROWS, 4 * HD), BF16),
            pltpu.VMEM((HEADS, SPAN, 2 * HD), BF16),
            pltpu.VMEM((HEADS, SPAN, 2 * HD), BF16),
            pltpu.VMEM((HEADS, SPAN, 2 * HD), BF16),
            pltpu.VMEM((HEADS, ROWS, 3 * HD), BF16),
            pltpu.VMEM((HEADS, WIDE_SLOTS, 3 * HD), BF16),
            pltpu.VMEM((HEADS, WIDE_SLOTS, 3 * HD), BF16),
            pltpu.VMEM((HEADS, ROWS, 3 * HD), BF16),
            pltpu.VMEM((HEADS, ROWS, HD), F32),
            pltpu.VMEM((HEADS, ROWS, HD), F32),
            pltpu.VMEM((128, WIDE_SLOTS), BF16),
            pltpu.VMEM((8, ROWS), I32),
            pltpu.VMEM((ROWS, 128), I32),
            pltpu.VMEM((HEADS, 8, WIDE_SLOTS), I32),
            pltpu.VMEM((HEADS, WIDE_SLOTS, 128), I32),
            dma((HEADS, 4)),
            dma((HEADS, 3)),
            dma, dma, dma, dma,
            dma((HEADS,)), dma((HEADS,)), dma((HEADS,)), dma((HEADS,)),
            dma((HEADS,)), dma((HEADS,)), dma((HEADS,)), dma((HEADS,)),
        ],
        compiler_params=pltpu.CompilerParams(
            collective_id=1, has_side_effects=True, vmem_limit_bytes=60 * 1024 * 1024
        ),
    )(*args)


def hand_over(*refs):
    held, in_sem, out_sem = refs[6:]
    pieces = [(t, p) for p in range(4) for t in range(3)]

    def move(t, p, inward):
        part = pl.ds(p * (ROWS // 4), ROWS // 4)
        if inward:
            return pltpu.make_async_copy(refs[t].at[part], held.at[t, part], in_sem.at[t, p])
        return pltpu.make_async_copy(held.at[t, part], refs[t + 3].at[part], out_sem.at[t, p])

    for t, p in pieces:
        move(t, p, True).start()
    for t, p in pieces:
        move(t, p, True).wait()
        move(t, p, False).start()
    for t, p in pieces:
        move(t, p, False).wait()


def call_hand_over(grads):
    hbm = pl.BlockSpec(memory_space=pl.ANY)
    grad = jax.ShapeDtypeStruct((ROWS, HEADS * HD), BF16)
    return pl.pallas_call(
        hand_over, out_shape=(grad, grad, grad), in_specs=[hbm] * 3, out_specs=(hbm, hbm, hbm),
        scratch_shapes=[
            pltpu.VMEM((3, ROWS, HEADS * HD), BF16),
            pltpu.SemaphoreType.DMA((3, 4)),
            pltpu.SemaphoreType.DMA((3, 4)),
        ],
    )(*grads)


def local(cluster_id, queries, key_vectors, value_vectors, grad_output):
    args = (cluster_id.reshape(1, 128), queries, key_vectors, value_vectors, grad_output)
    dq, dk, dv, flag = call_kernel(args)
    grads = lax.cond(
        flag[0, 0] > 0.5, lambda given, done: call_wide(given), lambda given, done: done,
        args, (dq, dk, dv),
    )
    return call_hand_over(grads)


def solution(mesh):
    placed = (P(("seq", "head")),) + (P("seq", "head"),) * 4
    return jax.shard_map(
        local,
        mesh=mesh,
        in_specs=placed,
        out_specs=(P("seq", "head"),) * 3,
        check_vma=False,
    )
```

profile of v0, /device:TPU:8, one launch (start us, length us, event | category | flops | bytes accessed | tf_op | source)
XLA Modules:
  0.0 239.0 jit_solution(6679494362992829988)
XLA Ops:
  0.6 0.0 copy-start.3
  0.6 0.6 copy-done.3
  1.3 0.0 copy-start
  1.3 0.0 copy-start.1
  1.3 0.0 copy-start.2
  1.3 234.0 %shard_map.76 = (bf16[1024,512]{1,0:T(8,128)(2,1)}, bf16[1024,512]{1,0:T(8,128)(2,1)}, bf16[1024,512]{1,0:T(8,128)(2,1)}, f32[1,1]{1,0:T(1,128)}) custom-call(s32[1,128]{1,0:T(1,128)S(1)} %bitcast.2, bf16[1024,512]{1,0:T(8,128)(2,1)} %q_ref.1, bf16[1024,512]{1,0:T(8,128)(2,1)} %k_ref.1, bf16[1024,512]{1,0:T(8,128)(2,1)} %v_ref.1, bf16[1024,512]{1,0:T(8,128)(2,1)} %g_ref.1), custom_call_target="tpu_custom_call" | custom-call | tf_op jit(solution)/shard_map/pallas_call | solution.py:989
  235.8 0.0 copy-done
  235.8 0.0 copy-done.1
  235.8 0.0 copy-done.2
  235.9 0.2 conditional.1
  236.0 2.8 %shard_map.77 = (bf16[1024,512]{1,0:T(8,128)(2,1)}, bf16[1024,512]{1,0:T(8,128)(2,1)}, bf16[1024,512]{1,0:T(8,128)(2,1)}) custom-call(bf16[1024,512]{1,0:T(8,128)(2,1)} %get-tuple-element.35.refs_0_, bf16[1024,512]{1,0:T(8,128)(2,1)} %get-tuple-element.36.refs_1_, bf16[1024,512]{1,0:T(8,128)(2,1)} %get-tuple-element.37.refs_2_), custom_call_target="tpu_custom_call" | custom-call | tf_op jit(solution)/shard_map/pallas_call | solution.py:1098
Async XLA Ops:
  0.6 0.7 copy-start.3
  1.3 234.5 %copy-start = (bf16[1024,512]{1,0:T(8,128)(2,1)S(1)}, bf16[1024,512]{1,0:T(8,128)(2,1)}, u32[]{:S(2)}) copy-start(bf16[1024,512]{1,0:T(8,128)(2,1)} %q_ref.1) | copy-start | bytes 3145732
  1.3 234.5 %copy-start.1 = (bf16[1024,512]{1,0:T(8,128)(2,1)S(1)}, bf16[1024,512]{1,0:T(8,128)(2,1)}, u32[]{:S(2)}) copy-start(bf16[1024,512]{1,0:T(8,128)(2,1)} %k_ref.1) | copy-start | bytes 3145732
  1.3 234.6 %copy-start.2 = (bf16[1024,512]{1,0:T(8,128)(2,1)S(1)}, bf16[1024,512]{1,0:T(8,128)(2,1)}, u32[]{:S(2)}) copy-start(bf16[1024,512]{1,0:T(8,128)(2,1)} %v_ref.1) | copy-start | bytes 3145732
where the time goes:
time: 239 us
  Pallas kernels  237 us (99%)
    pallas_call x1, Pallas kernels, call_kernel(): pl.pallas_call(kernel, out_shape=(grad, grad, grad, jax.ShapeDtypeStruct(...  234 us

commit v1 on v0

--- a/solution.py
+++ b/solution.py
@@ -653,17 +653,17 @@
             pack_forward(i + 2)
             stage_c(i + 2)
 
+        @pl.when(jnp.logical_and(i >= 3, i < HEADS + 2))
+        def _():
+            back_b(i - 3)
+
+        @pl.when(jnp.logical_and(i >= 2, i < HEADS + 2))
+        def _():
+            close_chunk(i - 2)
+
         @pl.when(i < HEADS)
         def _():
             last_span(i)
-
-        @pl.when(jnp.logical_and(i >= 3, i < HEADS + 2))
-        def _():
-            back_b(i - 3)
-
-        @pl.when(jnp.logical_and(i >= 2, i < HEADS + 2))
-        def _():
-            close_chunk(i - 2)
 
         @pl.when(i >= 4)
         def _():

time: 239 us -> 239 us (level)
  no operation moved by 1% of the time
where the time goes in v1:
time: 239 us; the launch traced here: 238 us
  Pallas kernels  236 us (99%)
    pallas_call x1, Pallas kernels, call_kernel(): pl.pallas_call(kernel, out_shape=(grad, grad, grad, jax.ShapeDtypeStruct(...  233 us

profile of v1, /device:TPU:8, one launch (start us, length us, event | category | flops | bytes accessed | tf_op | source)
XLA Modules:
  0.0 238.4 jit_solution(1176856983450406347)
XLA Ops:
  0.6 0.0 copy-start.3
  0.6 0.6 copy-done.3
  1.3 0.0 copy-start
  1.3 0.0 copy-start.1
  1.3 0.0 copy-start.2
  1.3 233.3 %shard_map.76 = (bf16[1024,512]{1,0:T(8,128)(2,1)}, bf16[1024,512]{1,0:T(8,128)(2,1)}, bf16[1024,512]{1,0:T(8,128)(2,1)}, f32[1,1]{1,0:T(1,128)}) custom-call(s32[1,128]{1,0:T(1,128)S(1)} %bitcast.2, bf16[1024,512]{1,0:T(8,128)(2,1)} %q_ref.1, bf16[1024,512]{1,0:T(8,128)(2,1)} %k_ref.1, bf16[1024,512]{1,0:T(8,128)(2,1)} %v_ref.1, bf16[1024,512]{1,0:T(8,128)(2,1)} %g_ref.1), custom_call_target="tpu_custom_call" | custom-call | tf_op jit(solution)/shard_map/pallas_call | solution.py:989
  235.2 0.0 copy-done
  235.2 0.0 copy-done.1
  235.2 0.0 copy-done.2
  235.2 0.2 conditional.1
  235.4 2.8 %shard_map.77 = (bf16[1024,512]{1,0:T(8,128)(2,1)}, bf16[1024,512]{1,0:T(8,128)(2,1)}, bf16[1024,512]{1,0:T(8,128)(2,1)}) custom-call(bf16[1024,512]{1,0:T(8,128)(2,1)} %get-tuple-element.35.refs_0_, bf16[1024,512]{1,0:T(8,128)(2,1)} %get-tuple-element.36.refs_1_, bf16[1024,512]{1,0:T(8,128)(2,1)} %get-tuple-element.37.refs_2_), custom_call_target="tpu_custom_call" | custom-call | tf_op jit(solution)/shard_map/pallas_call | solution.py:1098
Async XLA Ops:
  0.6 0.7 copy-start.3
  1.3 233.9 %copy-start = (bf16[1024,512]{1,0:T(8,128)(2,1)S(1)}, bf16[1024,512]{1,0:T(8,128)(2,1)}, u32[]{:S(2)}) copy-start(bf16[1024,512]{1,0:T(8,128)(2,1)} %q_ref.1) | copy-start | bytes 3145732
  1.3 233.9 %copy-start.1 = (bf16[1024,512]{1,0:T(8,128)(2,1)S(1)}, bf16[1024,512]{1,0:T(8,128)(2,1)}, u32[]{:S(2)}) copy-start(bf16[1024,512]{1,0:T(8,128)(2,1)} %k_ref.1) | copy-start | bytes 3145732
  1.3 233.9 %copy-start.2 = (bf16[1024,512]{1,0:T(8,128)(2,1)S(1)}, bf16[1024,512]{1,0:T(8,128)(2,1)}, u32[]{:S(2)}) copy-start(bf16[1024,512]{1,0:T(8,128)(2,1)} %v_ref.1) | copy-start | bytes 3145732
